TPU v7x, 128 devices: a whole 4x4x4 slice. The times are simulated.
128 devices in a mesh: slot: 32 (over x, y, core), ulysses: 4 (over z).
Axes of the slice: x: 4, y: 4, z: 4, core: 2. Of those that a mesh axis runs over, the one named last changes fastest.
Arguments:
- queries: bfloat16 [32768, 3072], P(('slot', 'ulysses')), may hold values from -6 to 6
- key_states: bfloat16 [32768, 3072], P(('slot', 'ulysses')), may hold values from -6 to 6
- value_states: bfloat16 [32768, 3072], P(('slot', 'ulysses')), may hold values from -3.5 to 3.5
- query_gain: float32 [128], replicated, may hold values from 0.1 to 1.9
- key_gain: float32 [128], replicated, may hold values from 0.1 to 1.9
- level_gate: float32 [16, 3072], replicated, may hold values from 0.3 to 1.5
- levels: int32 [32], replicated, may hold values from 0 to 15
- lengths: int32 [32], replicated, may hold values from 512 to 1024, as said below
- context: int32 [32], replicated, may hold values from 0 to 3, as said below
Outputs:
- gated: bfloat16 [32768, 3072], P(('slot', 'ulysses'))
Inputs may be any that keep to these rules, and one draw needn't show every extreme that they name: `lengths`: each group uses at least 512 of its token slots; some group uses all 1024. `context`: group c attends to at most c earlier groups; some group attends to 3.
All inputs are finite; a program needn't handle non-finite values.
Results may differ from a plain program's by a relative error of at most 0.0051.
Values may be sent and summed in bfloat16 or wider, within the bound.
A program may use at most 128 MiB of HBM per device.

v0:
```python
import functools
import math

import jax
import jax.numpy as jnp
from jax import lax
from jax.experimental import pallas as pl
from jax.experimental.pallas import tpu as pltpu
from jax.sharding import PartitionSpec as P

HD = 128
CORES = 2
CUTS = 2
MESH = pl.DeviceIdType.MESH
FACTOR = math.log2(math.e) / math.sqrt(HD)
F32, BF16 = jnp.float32, jnp.bfloat16


def kernel(
    slots, depth, levels_hbm, lengths_hbm, context_hbm, query_gain_hbm, key_gain_hbm, gate_hbm,
    q_hbm, k_hbm, v_hbm, out_hbm,
    levels, lengths, context, query_gain, key_gain, gate, q_in, k_in, v_in, q_own, k_own, v_own, q_far, local, ahead, part, part_sum, back, back_sum, done,
    load_sem, in_send, in_recv, q_send, q_recv, part_send, part_recv, out_send, out_recv,
):
    slot, z = lax.axis_index("slot"), lax.axis_index("ulysses")
    chip, core = slot // CORES, slot % CORES
    chips = slots // CORES
    heads = q_own.shape[0]
    span = q_own.shape[2]
    rows = span // depth
    mine = z * CORES + core
    partners = depth * CORES
    cuts = part_sum.shape[2]
    piece = span // cuts

    def chip_at(distance):
        return ((chip + distance + chips) % chips) * CORES + core, z

    def partner(r):
        return chip * CORES + (core + r % CORES) % CORES, (z + r // CORES) % depth

    loads = [
        pltpu.make_async_copy(source, target, load_sem.at[i])
        for i, (source, target) in enumerate((
            (lengths_hbm, lengths), (query_gain_hbm, query_gain), (key_gain_hbm, key_gain),
            (q_hbm, q_in), (k_hbm, k_in), (v_hbm, v_in),
            (context_hbm, context), (levels_hbm, levels), (gate_hbm, gate),
        ))
    ]
    for load in loads:
        load.start()

    barrier = pltpu.get_barrier_semaphore()
    everyone = [partner(r) for r in range(1, partners)] + [chip_at(d) for d in (-1, 1)]
    for other in everyone:
        pl.semaphore_signal(barrier, inc=1, device_id=other, device_id_type=MESH)

    def group(distance):
        return (chip * CORES + distance) % slots

    loads[0].wait()
    for g in range(CORES):
        used = lax.broadcasted_iota(jnp.int32, (span, HD), 0) < lengths[group(g)]
        ones = jnp.where(used, 1.0, 0.0).astype(BF16)
        for j in range(heads):
            v_own[j, g, :, HD:] = ones

    for load in loads[1:]:
        load.wait()
    pl.semaphore_wait(barrier, len(everyone))

    def columns(owner, j):
        return pl.ds(pl.multiple_of((owner * heads + j) * HD, HD), HD)

    own_rows = pl.ds(pl.multiple_of(z * rows, rows), rows)

    def normalize(ref, cols, gain):
        full = ref[:, cols].astype(F32)
        square = jnp.mean(full * full, axis=-1, keepdims=True)
        ref[:, cols] = (full * lax.rsqrt(square + 1e-06) * gain[...]).astype(BF16)

    def clip_values(cols):
        place = lax.broadcasted_iota(jnp.int32, (rows, HD), 0) + z * rows
        v_in[:, cols] = jnp.where(place < lengths[slot], v_in[:, cols].astype(F32), 0.0).astype(BF16)

    def landing(which, j, g):
        if which == 2:
            return v_own.at[j, g, :, pl.ds(0, HD)]
        return (q_own, k_own)[which].at[j, g]

    def send_in(which, j):
        source = (q_in, k_in, v_in)[which]
        if which == 2:
            target = v_own.at[j, core, own_rows, pl.ds(0, HD)]
        else:
            target = (q_own, k_own)[which].at[j, core, own_rows, :]

        def one(r, carry):
            to_slot, to_z = partner(r)
            cols = columns(to_z * CORES + to_slot % CORES, j)
            if which == 0:
                normalize(source, cols, query_gain)
            elif which == 1:
                normalize(source, cols, key_gain)
            else:
                clip_values(cols)

            @pl.when(r == 0)
            def _():
                pltpu.make_async_copy(source.at[:, cols], target, in_recv.at[which, j, core]).start()

            @pl.when(r > 0)
            def _():
                pltpu.make_async_remote_copy(
                    src_ref=source.at[:, cols], dst_ref=target,
                    send_sem=in_send.at[which, j], recv_sem=in_recv.at[which, j, core],
                    device_id=(to_slot, to_z), device_id_type=MESH,
                ).start()

            return carry

        lax.fori_loop(0, partners, one, 0)

    def await_in(which, j, g):
        here = landing(which, j, g)
        pltpu.make_async_copy(here, here, in_recv.at[which, j, g]).wait()

    asks = {0: chip > 0, 1: chip > 0, 2: (chip > 0) & (chip < chips - 1)}
    serves = {0: chip < chips - 1, 1: chip < chips - 1, 2: chip < chips - 2}
    merges = (chip > 0) & (chip < chips - 1)

    def rows_of(h):
        return pl.ds(h * piece, piece)

    def query_copy(j, n, h):
        source = q_far.at[j, 0] if n == 2 else q_own.at[j, n]
        return pltpu.make_async_remote_copy(
            src_ref=source.at[rows_of(h)], dst_ref=q_far.at[j, n, rows_of(h)],
            send_sem=q_send.at[j, n, h], recv_sem=q_recv.at[j, n, h],
            device_id=chip_at(-1), device_id_type=MESH,
        )

    def part_copies(j, n, h):
        return [
            pltpu.make_async_remote_copy(
                src_ref=source, dst_ref=target,
                send_sem=part_send.at[j, n, h, i], recv_sem=part_recv.at[j, n, h, i],
                device_id=chip_at(1), device_id_type=MESH,
            )
            for i, (source, target) in enumerate((
                (part.at[j, n, rows_of(h)], back.at[j, n, rows_of(h)]),
                (part_sum.at[j, n, h], back_sum.at[j, n, h]),
            ))
        ]

    def attend(queries, j, g):
        scores = lax.dot_general(
            queries, k_own[j, g], (((1,), (1,)), ((), ())), preferred_element_type=F32
        )
        weight = jnp.exp2(scores * FACTOR).astype(BF16)
        return jnp.dot(weight, v_own[j, g], preferred_element_type=F32)

    def allowed(distance, offset):
        return jnp.where(context[group(distance)] >= offset, 1.0, 0.0)

    diagonal = lax.broadcasted_iota(jnp.int32, (HD, HD), 0) == lax.broadcasted_iota(jnp.int32, (HD, HD), 1)

    def send_part(j, n, h, both, arrived):
        number = both[:, :HD]
        if arrived is not None:
            number = number + jnp.where(merges, back[j, arrived, rows_of(h), :].astype(F32), 0.0)
        part[j, n, rows_of(h), :] = number.astype(BF16)
        for s in range(piece // HD):
            total = both[s * HD:(s + 1) * HD, HD:]
            total = jnp.sum(jnp.where(diagonal, total, 0.0), axis=0, keepdims=True)
            if arrived is not None:
                total = total + jnp.where(merges, back_sum[j, arrived, h, s:s + 1, :], 0.0)
            part_sum[j, n, h, s:s + 1, :] = total
        for copy in part_copies(j, n, h):
            copy.start()

    def query_a_out(j):
        await_in(0, j, 0)

        @pl.when(asks[0])
        def _():
            for h in range(cuts):
                query_copy(j, 0, h).start()

    def query_b_out(j):
        await_in(0, j, 1)

        @pl.when(asks[1])
        def _():
            for h in range(cuts):
                query_copy(j, 1, h).start()

    def query_on(j):
        for h in range(cuts):

            @pl.when(serves[0])
            def _():
                query_copy(j, 0, h).wait_recv()

            @pl.when(asks[2])
            def _():
                query_copy(j, 2, h).start()

    def own_a(j):
        local[j, 0] = attend(q_own[j, 0], j, 0)

    def own_b(j):
        queries = q_own[j, 1]
        local[j, 1] = attend(queries, j, 1) + allowed(1, 1) * attend(queries, j, 0)

    def part_c(j):
        @pl.when(serves[2])
        def _():
            for h in range(cuts):
                query_copy(j, 2, h).wait_recv()
                both = allowed(4, 3) * attend(q_far[j, 2, rows_of(h), :], j, 1)
                send_part(j, 2, h, both, None)

    def part_b(j):
        @pl.when(serves[1])
        def _():
            for h in range(cuts):
                query_copy(j, 1, h).wait_recv()
                queries = q_far[j, 1, rows_of(h), :]
                both = allowed(3, 2) * attend(queries, j, 1) + allowed(3, 3) * attend(queries, j, 0)
                send_part(j, 1, h, both, None)

    def part_a_begin(j):
        @pl.when(serves[0])
        def _():
            queries = q_far[j, 0]
            ahead[...] = allowed(2, 1) * attend(queries, j, 1) + allowed(2, 2) * attend(queries, j, 0)

    def part_a_end(j):
        for h in range(cuts):

            @pl.when(merges)
            def _():
                for copy in part_copies(j, 2, h):
                    copy.wait_recv()

            @pl.when(serves[0])
            def _():
                send_part(j, 0, h, ahead[rows_of(h), :], 2)

    def finish(j, g):
        levels_here = lax.broadcasted_iota(jnp.int32, (gate.shape[0], HD), 0) == levels[group(g)]
        gate_row = jnp.sum(jnp.where(levels_here, gate[:, columns(mine, j)], 0.0), axis=0, keepdims=True)
        target = out_hbm.at[:, columns(mine, j)]
        to_slot = chip * CORES + g
        for h in range(cuts):

            @pl.when(chip > 0)
            def _():
                for copy in part_copies(j, g, h):
                    copy.wait_recv()

            for s in range(piece // HD):
                first = h * piece + s * HD
                here = pl.ds(first, HD)
                both = local[j, g, here, :]
                number = both[:, :HD] + jnp.where(chip > 0, back[j, g, here, :].astype(F32), 0.0)
                total = jnp.where(chip > 0, back_sum[j, g, h, s:s + 1, :], 0.0)
                total = both[:, HD:] + jnp.broadcast_to(total, (HD, HD)).T
                place = lax.broadcasted_iota(jnp.int32, (HD, HD), 0) + first
                attended = jnp.where(place < lengths[group(g)], number / total, 0.0).astype(BF16)
                done[j, g, here, :] = (gate_row * attended.astype(F32)).astype(BF16)
            for to_z in range(h * depth // cuts, (h + 1) * depth // cuts):
                source = done.at[j, g, pl.ds(to_z * rows, rows), :]

                @pl.when((to_slot == slot) & (to_z == z))
                def _():
                    pltpu.make_async_copy(source, target, out_recv.at[j]).start()

                @pl.when((to_slot != slot) | (to_z != z))
                def _():
                    pltpu.make_async_remote_copy(
                        src_ref=source, dst_ref=target, send_sem=out_send.at[j], recv_sem=out_recv.at[j],
                        device_id=(to_slot, to_z), device_id_type=MESH,
                    ).start()

    def keys_in(j, g):
        await_in(1, j, g)
        await_in(2, j, g)

    def heads_in(j):
        @pl.when(core == 0)
        def _():
            for which in (0, 1, 2):
                send_in(which, j)

        @pl.when(core != 0)
        def _():
            for which in (1, 2, 0):
                send_in(which, j)

    last = heads - 1
    for j in range(heads):
        heads_in(j)
        if j == 0:
            query_a_out(0)
    query_on(0)
    for j in range(last):
        keys_in(j, 1)
        if j > 0:
            query_b_out(j)
        part_c(j)
        if j == 0:
            query_b_out(j)
        keys_in(j, 0)
        part_a_begin(j)
        query_a_out(j + 1)
        own_a(j)
        part_a_end(j)
        part_b(j)
        query_on(j + 1)
        own_b(j)
    keys_in(last, 1)
    query_b_out(last)
    keys_in(last, 0)
    part_a_begin(last)
    for j in range(last - 1):
        finish(j, 0)
        finish(j, 1)
    own_a(last)
    part_c(last)
    finish(last - 1, 0)
    part_a_end(last)
    finish(last - 1, 1)
    part_b(last)
    own_b(last)
    finish(last, 0)
    finish(last, 1)

    sent = q_in.at[:, pl.ds(0, (partners - 1) * HD)]
    got = q_in.at[:, pl.ds(0, partners * HD)]
    for j in range(heads):
        pltpu.make_async_copy(got, got, out_recv.at[j]).wait()
        pltpu.make_async_copy(sent, sent, out_send.at[j]).wait()
        for which in range(3):
            pltpu.make_async_copy(sent, sent, in_send.at[which, j]).wait()
        for n in range(3):
            for h in range(cuts):

                @pl.when(asks[n])
                def _():
                    query_copy(j, n, h).wait_send()

                @pl.when(serves[n])
                def _():
                    for copy in part_copies(j, n, h):
                        copy.wait_send()


def attention(slots, depth, levels, lengths, context, query_gain, key_gain, level_gate, queries, key_states, value_states):
    rows, width = queries.shape
    heads = width // (HD * depth * CORES)
    span = rows * depth
    row = pltpu.VMEM((rows, width), BF16)
    cuts = CUTS
    lines = (heads, 3, cuts, span // cuts // HD, HD)
    dma = pltpu.SemaphoreType.DMA
    return pl.pallas_call(
        functools.partial(kernel, slots, depth),
        out_shape=jax.ShapeDtypeStruct((rows, width), BF16),
        in_specs=[pl.BlockSpec(memory_space=pl.ANY)] * 9,
        out_specs=pl.BlockSpec(memory_space=pl.ANY),
        scratch_shapes=[
            pltpu.SMEM(levels.shape, jnp.int32), pltpu.SMEM(lengths.shape, jnp.int32),
            pltpu.SMEM(context.shape, jnp.int32),
            pltpu.VMEM((1, HD), F32), pltpu.VMEM((1, HD), F32), pltpu.VMEM(level_gate.shape, F32),
            row, row, row,
            pltpu.VMEM((heads, CORES, span, HD), BF16),
            pltpu.VMEM((heads, CORES, span, HD), BF16),
            pltpu.VMEM((heads, CORES, span, 2 * HD), BF16),
            pltpu.VMEM((heads, 3, span, HD), BF16),
            pltpu.VMEM((heads, CORES, span, 2 * HD), F32),
            pltpu.VMEM((span, 2 * HD), F32),
            pltpu.VMEM((heads, 3, span, HD), BF16),
            pltpu.VMEM(lines, F32),
            pltpu.VMEM((heads, 3, span, HD), BF16),
            pltpu.VMEM(lines, F32),
            pltpu.VMEM((heads, CORES, span, HD), BF16),
            dma((9,)), dma((3, heads)), dma((3, heads, CORES)), dma((heads, 3, cuts)), dma((heads, 3, cuts)),
            dma((heads, 3, cuts, 2)), dma((heads, 3, cuts, 2)), dma((heads,)), dma((heads,)),
        ],
        compiler_params=pltpu.CompilerParams(
            collective_id=0, has_side_effects=True, vmem_limit_bytes=60 * 2**20
        ),
        cost_estimate=pl.CostEstimate(
            flops=32 * heads * span * span * HD, bytes_accessed=8 * rows * width,
            transcendentals=8 * heads * span * span,
        ),
    )(
        levels, lengths, context, query_gain[None, :], key_gain[None, :], level_gate,
        queries, key_states, value_states,
    )


def shards(
    slots, depth, queries, key_states, value_states, query_gain, key_gain, level_gate, levels, lengths, context
):
    return attention(
        slots, depth, levels, lengths, context, query_gain, key_gain, level_gate,
        queries, key_states, value_states,
    )


def solution(mesh):
    split = P(("slot", "ulysses"), None)
    return jax.shard_map(
        functools.partial(shards, mesh.shape["slot"], mesh.shape["ulysses"]),
        mesh=mesh,
        in_specs=(split, split, split) + (P(),) * 6,
        out_specs=split,
        check_vma=False,
    )
```

profile of v0, /device:TPU:7, one launch (start us, length us, event | category | flops | bytes accessed | tf_op | source)
XLA Modules:
  0.0 93.1 jit_solution(2957052450424095208)
XLA Ops:
  0.0 90.4 %shard_map.91 = bf16[256,3072]{1,0:T(8,128)(2,1)} custom-call(s32[32]{0:T(128)} %levels_hbm.1, s32[32]{0:T(128)} %lengths_hbm.1, s32[32]{0:T(128)} %context_hbm.1, f32[1,128]{1,0:T(1,128)} %bitcast.2, f32[1,128]{1,0:T(1,128)} %bitcast.3, f32[16,3072]{1,0:T(8,128)} %gate_hbm.1, bf16[256,3072]{1,0:T(8,128)(2,1)} %q_hbm.1, bf16[256,3072]{1,0:T(8,128)(2,1)} %k_hbm.1, ...), custom_call_target="tpu_custom_call" | custom-call | flops 12884901888 | bytes 6291456 | tf_op jit(solution)/shard_map/pallas_call | solution.py:368
  90.4 2.7 %copy.11 = bf16[256,3072]{1,0:T(8,128)(2,1)} copy(bf16[256,3072]{1,0:T(8,128)(2,1)} %shard_map.91) | data formatting | bytes 3145728
where the time goes:
time: 93.2 us; the launch traced here: 93.1 us
  Pallas kernels  90.4 us (97%)
  local copies, waits for them, and re-layouts  2.65 us (3%)
    pallas_call x1, Pallas kernels, attention(): pl.pallas_call(functools.partial(kernel, slots, depth), out_shape=jax.Sha...  90.4 us
    unnamed x1, local copies, waits for them, and re-layouts  2.65 us

commit v1 on v0

--- a/solution.py
+++ b/solution.py
@@ -367,7 +367,7 @@
     dma = pltpu.SemaphoreType.DMA
     return pl.pallas_call(
         functools.partial(kernel, slots, depth),
-        out_shape=jax.ShapeDtypeStruct((rows, width), BF16),
+        out_shape=pltpu.VMEM((rows, width), BF16),
         in_specs=[pl.BlockSpec(memory_space=pl.ANY)] * 9,
         out_specs=pl.BlockSpec(memory_space=pl.ANY),
         scratch_shapes=[
@@ -390,7 +390,7 @@
             dma((heads, 3, cuts, 2)), dma((heads, 3, cuts, 2)), dma((heads,)), dma((heads,)),
         ],
         compiler_params=pltpu.CompilerParams(
-            collective_id=0, has_side_effects=True, vmem_limit_bytes=60 * 2**20
+            collective_id=0, has_side_effects=True, vmem_limit_bytes=54 * 2**20
         ),
         cost_estimate=pl.CostEstimate(
             flops=32 * heads * span * span * HD, bytes_accessed=8 * rows * width,

time: 93.2 us -> 91.6 us (0.983)
  local copies, waits for them, and re-layouts: 2.65 us -> 1.15 us
    unnamed x1, local copies, waits for them, and re-layouts: 2.65 us -> 1.15 us
where the time goes in v1:
time: 91.6 us; the launch traced here: 91.5 us
  Pallas kernels  90.3 us (99%)
  local copies, waits for them, and re-layouts  1.15 us (1%)
    pallas_call x1, Pallas kernels, attention(): pl.pallas_call(functools.partial(kernel, slots, depth), out_shape=pltpu.V...  90.3 us

profile of v1, /device:TPU:7, one launch (start us, length us, event | category | flops | bytes accessed | tf_op | source)
XLA Modules:
  0.0 91.5 jit_solution(17249915422699132518)
XLA Ops:
  0.0 90.3 %shard_map.91 = bf16[256,3072]{1,0:T(8,128)(2,1)S(1)} custom-call(s32[32]{0:T(128)} %levels_hbm.1, s32[32]{0:T(128)} %lengths_hbm.1, s32[32]{0:T(128)} %context_hbm.1, f32[1,128]{1,0:T(1,128)} %bitcast.2, f32[1,128]{1,0:T(1,128)} %bitcast.3, f32[16,3072]{1,0:T(8,128)} %gate_hbm.1, bf16[256,3072]{1,0:T(8,128)(2,1)} %q_hbm.1, bf16[256,3072]{1,0:T(8,128)(2,1)} %k_hbm.1, ...), custom_call_target="tpu_custom_call" | custom-call | flops 12884901888 | bytes 6291456 | tf_op jit(solution)/shard_map/pallas_call | solution.py:368
  90.3 1.1 %copy.11 = bf16[256,3072]{1,0:T(8,128)(2,1)} copy(bf16[256,3072]{1,0:T(8,128)(2,1)S(1)} %shard_map.91) | data formatting | bytes 3145728

commit v2 on v1

--- a/solution.py
+++ b/solution.py
@@ -176,7 +176,7 @@
             if arrived is not None:
                 total = total + jnp.where(merges, back_sum[j, arrived, h, s:s + 1, :], 0.0)
             part_sum[j, n, h, s:s + 1, :] = total
-        for copy in part_copies(j, n, h):
+        for copy in reversed(part_copies(j, n, h)):
             copy.start()
 
     def query_a_out(j):
@@ -296,7 +296,7 @@
 
         @pl.when(core != 0)
         def _():
-            for which in (1, 2, 0):
+            for which in (1, 2, 0) if j == 0 else (0, 1, 2):
                 send_in(which, j)
 
     last = heads - 1
@@ -307,8 +307,6 @@
     query_on(0)
     for j in range(last):
         keys_in(j, 1)
-        if j > 0:
-            query_b_out(j)
         part_c(j)
         if j == 0:
             query_b_out(j)
@@ -319,9 +317,9 @@
         part_a_end(j)
         part_b(j)
         query_on(j + 1)
+        query_b_out(j + 1)
         own_b(j)
     keys_in(last, 1)
-    query_b_out(last)
     keys_in(last, 0)
     part_a_begin(last)
     for j in range(last - 1):
@@ -331,8 +329,8 @@
     part_c(last)
     finish(last - 1, 0)
     part_a_end(last)
+    part_b(last)
     finish(last - 1, 1)
-    part_b(last)
     own_b(last)
     finish(last, 0)
     finish(last, 1)

time: 91.6 us -> 91.5 us (level)
  no operation moved by 1% of the time
where the time goes in v2:
time: 91.5 us; the launch traced here: 91.4 us
  Pallas kernels  90.3 us (99%)
  local copies, waits for them, and re-layouts  1.15 us (1%)
    pallas_call x1, Pallas kernels, attention(): pl.pallas_call(functools.partial(kernel, slots, depth), out_shape=pltpu.V...  90.3 us

profile of v2, /device:TPU:7, one launch (start us, length us, event | category | flops | bytes accessed | tf_op | source)
XLA Modules:
  0.0 91.4 jit_solution(3916120854842175022)
XLA Ops:
  0.0 90.3 %shard_map.91 = bf16[256,3072]{1,0:T(8,128)(2,1)S(1)} custom-call(s32[32]{0:T(128)} %levels_hbm.1, s32[32]{0:T(128)} %lengths_hbm.1, s32[32]{0:T(128)} %context_hbm.1, f32[1,128]{1,0:T(1,128)} %bitcast.2, f32[1,128]{1,0:T(1,128)} %bitcast.3, f32[16,3072]{1,0:T(8,128)} %gate_hbm.1, bf16[256,3072]{1,0:T(8,128)(2,1)} %q_hbm.1, bf16[256,3072]{1,0:T(8,128)(2,1)} %k_hbm.1, ...), custom_call_target="tpu_custom_call" | custom-call | flops 12884901888 | bytes 6291456 | tf_op jit(solution)/shard_map/pallas_call | solution.py:366
  90.3 1.1 %copy.11 = bf16[256,3072]{1,0:T(8,128)(2,1)} copy(bf16[256,3072]{1,0:T(8,128)(2,1)S(1)} %shard_map.91) | data formatting | bytes 3145728
